TPU v7x, 32 devices: a whole 2x2x4 slice. The times are simulated.
32 devices in a mesh: grp: 2 (over x), exp: 8 (over z, y), sp: 2 (over core).
Axes of the slice: x: 2, y: 2, z: 4, core: 2. Of those that a mesh axis runs over, the one named last changes fastest.
Arguments:
- tokens: bfloat16 [2048, 2560], P(('grp', 'exp')), parts along dimension 0, may hold values from -6 to 6
- cotangent: bfloat16 [2048, 2560], P(('grp', 'exp')), parts along dimension 0, may hold values from -0.59765625 to 0.59765625
- expert_ids: int32 [2048, 6], P(('grp', 'exp')), parts along dimension 0, may hold values from 0 to 7, as said below
- slot_ids: int32 [2048, 6], P(('grp', 'exp')), parts along dimension 0, may hold values from 0 to 119, as said below
- gates: float32 [2048, 6], P(('grp', 'exp')), parts along dimension 0, may hold values from 0.1 to 4
- w_gate: bfloat16 [8, 2560, 768], P('exp', None, 'sp'), may hold values from -0.125 to 0.125
- w_up: bfloat16 [8, 2560, 768], P('exp', None, 'sp'), may hold values from -0.125 to 0.125
- w_down: bfloat16 [8, 2560, 768], P('exp', None, 'sp'), may hold values from -0.21875 to 0.21875
- s_gate: bfloat16 [2560, 1536], P('exp', 'sp'), may hold values from -0.125 to 0.125
- s_up: bfloat16 [2560, 1536], P('exp', 'sp'), may hold values from -0.125 to 0.125
- s_down: bfloat16 [2560, 1536], P('exp', 'sp'), may hold values from -0.15625 to 0.15625
Outputs:
- input_grad: bfloat16 [2048, 2560], P(('grp', 'exp'), 'sp'), parts along dimension 0
- gate_grads: float32 [2048, 6], P(('grp', 'exp'), 'sp'), parts along dimension 0
There are 2 independent parts, one for each index of `grp`. A program takes and returns all parts, laid end to end along the dimension named above; an argument that names none is the same for every part. Nothing has to cross between parts.
Inputs may be any that keep to these rules, and one draw needn't show every extreme that they name: `expert_ids`: each row names 6 different experts. In each aligned block of 128 rows (the rows of one index of exp) no expert is named by more than 120 rows; in every block one expert, the same in all blocks of a group, and one more are named by exactly 120 rows, and every expert by at least one. `slot_ids`: within each aligned block of 128 rows, the rows that name one expert hold the slots 0 to their count - 1 for it, each once.
All inputs are finite; a program needn't handle non-finite values.
Results may differ from a plain program's by a relative error of at most 0.0057.
Values may be sent and summed in bfloat16 or wider, within the bound.
A program may use at most 128 MiB of HBM per device.

v0:
```python
import jax
import jax.numpy as jnp
from jax import lax
from jax.sharding import PartitionSpec as P


def swiglu_grads(gate_pre, up_pre, grad_out):
    sigmoid_val = jax.nn.sigmoid(gate_pre)
    silu_val = gate_pre * sigmoid_val
    grad_gate = grad_out * up_pre * sigmoid_val * (1.0 + gate_pre * (1.0 - sigmoid_val))
    grad_up = grad_out * silu_val
    return (grad_gate.astype(jnp.bfloat16), grad_up.astype(jnp.bfloat16), silu_val * up_pre)


def contract_back(grads, weight):
    return lax.dot_general(
        grads, weight, (((1,), (1,)), ((), ())), preferred_element_type=jnp.float32
    )


def run_experts(arrived_x, arrived_dy, w_gate, w_up, w_down):
    local_count = w_gate.shape[0]
    slot_count = arrived_x.shape[1]
    source_count = arrived_x.shape[0] // local_count

    def regroup(values):
        shaped = values.reshape((source_count, local_count) + values.shape[1:])
        return jnp.swapaxes(shaped, 0, 1).reshape(
            (local_count, source_count * slot_count) + values.shape[2:]
        )

    def ungroup(values):
        shaped = values.reshape((local_count, source_count, slot_count) + values.shape[2:])
        return jnp.swapaxes(shaped, 0, 1).reshape(
            (source_count * local_count, slot_count) + values.shape[2:]
        )

    rows_x = regroup(arrived_x)
    rows_dy = regroup(arrived_dy)
    gate_pre = jnp.einsum("erd,edh->erh", rows_x, w_gate, preferred_element_type=jnp.float32)
    up_pre = jnp.einsum("erd,edh->erh", rows_x, w_up, preferred_element_type=jnp.float32)
    grad_out = jnp.einsum("erd,edh->erh", rows_dy, w_down, preferred_element_type=jnp.float32)
    grad_gate, grad_up, hidden = swiglu_grads(gate_pre, up_pre, grad_out)
    part_gate = jnp.sum(grad_out * hidden, axis=2).astype(jnp.bfloat16)
    both_grads = jnp.concatenate([grad_gate, grad_up], axis=2)
    both_weights = jnp.concatenate([w_gate, w_up], axis=2)
    pieces = jnp.einsum(
        "erh,edh->erd", both_grads, both_weights, preferred_element_type=jnp.float32
    )
    return (ungroup(pieces.astype(jnp.bfloat16)), ungroup(part_gate))


def body(
    tokens, cotangent, expert_ids, slot_ids, gates, w_gate, w_up, w_down, s_gate, s_up, s_down
):
    row_count, feature_count = tokens.shape
    top_count = expert_ids.shape[1]
    experts = w_gate.shape[0] * lax.axis_size("exp")
    capacity = min(row_count, 2 * (5 * row_count * top_count // (8 * experts)))
    slot_table = expert_ids * capacity + slot_ids
    flat_index = slot_table.reshape(-1)
    token_number = jnp.broadcast_to(
        jnp.arange(row_count, dtype=jnp.int32)[:, None], (row_count, top_count)
    ).reshape(-1)
    slot_owner = jnp.zeros((experts * capacity,), jnp.int32).at[flat_index].set(token_number)
    send_x = jnp.take(tokens, slot_owner, axis=0).reshape(experts, capacity, feature_count)
    send_dy = jnp.take(cotangent, slot_owner, axis=0).reshape(experts, capacity, feature_count)
    full_gate, full_up, full_down = (
        lax.all_gather(s_gate, "exp", axis=0, tiled=True),
        lax.all_gather(s_up, "exp", axis=0, tiled=True),
        lax.all_gather(s_down, "exp", axis=0, tiled=True),
    )
    combined = jnp.zeros((row_count, feature_count), jnp.float32)
    arrived_x, arrived_dy = (
        lax.all_to_all(send_x, "exp", split_axis=0, concat_axis=0, tiled=True),
        lax.all_to_all(send_dy, "exp", split_axis=0, concat_axis=0, tiled=True),
    )
    pieces, part_gate = run_experts(arrived_x, arrived_dy, w_gate, w_up, w_down)
    returned, returned_gate = (
        lax.all_to_all(pieces, "exp", split_axis=0, concat_axis=0, tiled=True),
        lax.all_to_all(part_gate, "exp", split_axis=0, concat_axis=0, tiled=True),
    )
    flat_rows = returned.reshape(-1, feature_count)
    for column in range(top_count):
        picked = jnp.take(flat_rows, slot_table[:, column], axis=0)
        combined = combined + gates[:, column : column + 1] * picked.astype(jnp.float32)
    gate_part = (
        jnp.take(returned_gate.reshape(-1), flat_index)
        .reshape(row_count, top_count)
        .astype(jnp.float32)
    )
    gate_pre = jnp.dot(tokens, full_gate, preferred_element_type=jnp.float32)
    up_pre = jnp.dot(tokens, full_up, preferred_element_type=jnp.float32)
    grad_out = jnp.dot(cotangent, full_down, preferred_element_type=jnp.float32)
    grad_gate, grad_up, hidden = swiglu_grads(gate_pre, up_pre, grad_out)
    combined = combined + contract_back(grad_gate, full_gate) + contract_back(grad_up, full_up)
    dx_half, gate_half = (
        lax.psum_scatter(combined, "sp", scatter_dimension=1, tiled=True),
        lax.psum_scatter(gate_part, "sp", scatter_dimension=1, tiled=True),
    )
    return (dx_half.astype(jnp.bfloat16), gate_half)


def solution(mesh):
    in_specs = (
        P(("grp", "exp"), None),
        P(("grp", "exp"), None),
        P(("grp", "exp"), None),
        P(("grp", "exp"), None),
        P(("grp", "exp"), None),
        P("exp", None, "sp"),
        P("exp", None, "sp"),
        P("exp", None, "sp"),
        P("exp", "sp"),
        P("exp", "sp"),
        P("exp", "sp"),
    )
    out_specs = (P(("grp", "exp"), "sp"), P(("grp", "exp"), "sp"))
    return jax.shard_map(body, mesh=mesh, in_specs=in_specs, out_specs=out_specs, check_vma=False)
```

profile of v0, /device:TPU:0, one launch (start us, length us, event | category | flops | bytes accessed | tf_op | source)
XLA Modules:
  0.0 607.6 jit_solution(16098182896327542164)
XLA Ops:
  11.9 11.6 %gather_fusion.2 = bf16[960,2560]{1,0:T(8,128)(2,1)} fusion(bf16[128,2560]{1,0:T(8,128)(2,1)} %param.15, s32[1024]{0:T(1024)S(1)} %pad_clamp_fusion.7), kind=kCustom, calls=%fused_computation.2.clone | custom fusion | bytes 9834240 | tf_op jit(solution)/shard_map/jit(_take)/gather | solution.py:66
  23.5 6.2 %gather_fusion.1 = bf16[960,2560]{1,0:T(8,128)(2,1)} fusion(bf16[128,2560]{1,0:T(8,128)(2,1)S(1)} %copy-done.2, s32[1024]{0:T(1024)S(1)} %pad_clamp_fusion.7), kind=kCustom, calls=%fused_computation.clone | custom fusion | bytes 9834240 | tf_op jit(solution)/shard_map/jit(_take)/gather | solution.py:67
  29.7 8.6 %broadcast_select_fusion = (bf16[960,2560]{1,0:T(8,128)(2,1)}, bf16[960,2560]{1,0:T(8,128)(2,1)}) fusion(bf16[960,2560]{1,0:T(8,128)(2,1)} %gather_fusion.2, pred[960]{0:T(1024)(128)(4,1)S(1)} %compare_and_fusion, bf16[960,2560]{1,0:T(8,128)(2,1)} %gather_fusion.1), kind=kLoop, calls=%fused_computation.11 | loop fusion | flops 4915200 | bytes 19661760 | tf_op jit(solution)/shard_map/jit(_take)/select_n | solution.py:66
  38.3 7.3 %all-to-all-start.1 = ((bf16[8,120,2560]{2,1,0:T(8,128)(2,1)}), bf16[8,120,2560]{2,1,0:T(8,128)(2,1)}, u32[]{:S(2)}, u32[]{:S(2)}) async-start(bf16[8,120,2560]{2,1,0:T(8,128)(2,1)} %bitcast.72), calls=%async_computation.1 | async-start | bytes 9830400 | tf_op jit(solution)/shard_map/all_to_all | solution.py:75
  46.3 155.5 %all-to-all-done.1 = bf16[8,120,2560]{2,1,0:T(8,128)(2,1)} async-done(((bf16[8,120,2560]{2,1,0:T(8,128)(2,1)}), bf16[8,120,2560]{2,1,0:T(8,128)(2,1)}, u32[]{:S(2)}, u32[]{:S(2)}) %all-to-all-start.1) | async-done | bytes 4915232 | tf_op jit(solution)/shard_map/all_to_all | solution.py:75
  201.8 4.6 all-to-all-start
  207.2 7.1 %fusion.2 = f32[960,384]{1,0:T(8,128)} fusion(bf16[960,2560]{1,0:T(8,128)(2,1)} %bitcast.6, bf16[1,2560,384]{2,1,0:T(8,128)(2,1)} %param.20), kind=kOutput, calls=%fused_computation.18 | convolution fusion | flops 1887436800 | bytes 8355840 | tf_op jit(solution)/shard_map/erd,edh->erh/dot_general | solution.py:40
  214.3 6.2 %fusion.4 = f32[960,384]{1,0:T(8,128)} fusion(bf16[960,2560]{1,0:T(8,128)(2,1)} %bitcast.6, bf16[1,2560,384]{2,1,0:T(8,128)(2,1)S(1)} %copy-done.5), kind=kOutput, calls=%fused_computation.20 | convolution fusion | flops 1887436800 | bytes 8355840 | tf_op jit(solution)/shard_map/erd,edh->erh/dot_general | solution.py:41
  220.5 141.2 %all-to-all-done = bf16[8,120,2560]{2,1,0:T(8,128)(2,1)} async-done(((bf16[8,120,2560]{2,1,0:T(8,128)(2,1)}), bf16[8,120,2560]{2,1,0:T(8,128)(2,1)}, u32[]{:S(2)}, u32[]{:S(2)}) %all-to-all-start) | async-done | bytes 4915232 | tf_op jit(solution)/shard_map/all_to_all | solution.py:76
  361.8 6.7 %multiply_reduce_fusion = (bf16[960]{0:T(1024)(128)(2,1)S(1)}, bf16[1,960,384]{2,1,0:T(8,128)(2,1)S(1)}, bf16[1,960,384]{2,1,0:T(8,128)(2,1)S(1)}) fusion(f32[960,384]{1,0:T(8,128)} %fusion.4, f32[960,384]{1,0:T(8,128)} %fusion.2, bf16[960,2560]{1,0:T(8,128)(2,1)} %bitcast.3, bf16[1,2560,384]{2,1,0:T(8,128)(2,1)S(1)} %copy-done), kind=kOutput, calls=%fused_computation.27 | convolution fusion | flops 1893334016 | bytes 11306880 | tf_op jit(solution)/shard_map/erd,edh->erh/dot_general | solution.py:42
  368.5 5.8 convolution_convert_fusion
  374.3 4.8 all-to-all-start.2
  385.8 148.5 %all-to-all-done.2 = bf16[8,120,2560]{2,1,0:T(8,128)(2,1)} async-done(((bf16[8,120,2560]{2,1,0:T(8,128)(2,1)}), bf16[8,120,2560]{2,1,0:T(8,128)(2,1)}, u32[]{:S(2)}, u32[]{:S(2)}) %all-to-all-start.2) | async-done | bytes 4915232 | tf_op jit(solution)/shard_map/all_to_all | solution.py:80
  534.3 5.5 gather_fusion.3
  539.8 5.5 gather_fusion.4
  545.3 5.5 gather_fusion.5
  550.8 5.5 gather_fusion.6
  556.3 5.5 gather_fusion.7
  561.8 5.7 gather_fusion.8
  567.5 6.6 %convolution_add_fusion.1 = f32[128,2560]{1,0:T(8,128)S(1)} fusion(bf16[2560,768]{1,0:T(8,128)(2,1)} %all-gather.8.cloned.1.call-done, f32[128,768]{1,0:T(8,128)S(1)} %fusion.30, bf16[128,2560]{1,0:T(8,128)(2,1)S(1)} %copy-done.3, bf16[2560,768]{1,0:T(8,128)(2,1)} %all-gather.6.cloned.1.call-done, bf16[128,2560]{1,0:T(8,128)(2,1)} %gather_fusion.8, ...), kind=kOutput, calls=%fused_computation.17 | convolution fusion | flops 1015480320 | bytes 14552832 | tf_op jit(solution)/shard_map/dot_general | solution.py:16
  574.1 4.6 convolution_add_fusion
  584.2 5.1 all-to-all-done.3
  589.5 5.0 gather_fusion
  594.8 3.6 all-reduce
  (60 shorter events, 20.6 us)
Async XLA Ops:
  7.2 354.6 %copy-start = (bf16[1,2560,384]{2,1,0:T(8,128)(2,1)S(1)}, bf16[1,2560,384]{2,1,0:T(8,128)(2,1)}, u32[]{:S(2)}) copy-start(bf16[1,2560,384]{2,1,0:T(8,128)(2,1)} %param.22) | copy-start | bytes 5898244
  11.9 11.6 %copy-start.2 = (bf16[128,2560]{1,0:T(8,128)(2,1)S(1)}, bf16[128,2560]{1,0:T(8,128)(2,1)}, u32[]{:S(2)}) copy-start(bf16[128,2560]{1,0:T(8,128)(2,1)} %param.16) | copy-start | bytes 1966084
  38.3 163.6 %all-to-all-start.1 = ((bf16[8,120,2560]{2,1,0:T(8,128)(2,1)}), bf16[8,120,2560]{2,1,0:T(8,128)(2,1)}, u32[]{:S(2)}, u32[]{:S(2)}) async-start(bf16[8,120,2560]{2,1,0:T(8,128)(2,1)} %bitcast.72), calls=%async_computation.1 | async-start | bytes 9830400 | tf_op jit(solution)/shard_map/all_to_all | solution.py:75
  45.6 334.6 %all-gather.8.cloned.1.call-start = ((), (), s32[]{:S(2)}) async-start(), calls=%async_computation.7 | async-start | bytes 4423680 | tf_op jit(solution)/shard_map/all_gather | solution.py:69
  201.8 159.9 %all-to-all-start = ((bf16[8,120,2560]{2,1,0:T(8,128)(2,1)}), bf16[8,120,2560]{2,1,0:T(8,128)(2,1)}, u32[]{:S(2)}, u32[]{:S(2)}) async-start(bf16[8,120,2560]{2,1,0:T(8,128)(2,1)} %bitcast.71), calls=%async_computation | async-start | bytes 9830400 | tf_op jit(solution)/shard_map/all_to_all | solution.py:76
  206.5 176.5 %all-gather.4.cloned.1.call-start = ((), (), s32[]{:S(2)}) async-start(), calls=%async_computation.5 | async-start | bytes 4423680 | tf_op jit(solution)/shard_map/all_gather | solution.py:71
  207.2 7.1 %copy-start.5 = (bf16[1,2560,384]{2,1,0:T(8,128)(2,1)S(1)}, bf16[1,2560,384]{2,1,0:T(8,128)(2,1)}, u32[]{:S(2)}) copy-start(bf16[1,2560,384]{2,1,0:T(8,128)(2,1)} %param.21) | copy-start | bytes 5898244
  361.8 6.7 %copy-start.6 = (bf16[1,2560,384]{2,1,0:T(8,128)(2,1)S(1)}, bf16[1,2560,384]{2,1,0:T(8,128)(2,1)}, u32[]{:S(2)}) copy-start(bf16[1,2560,384]{2,1,0:T(8,128)(2,1)} %param.21) | copy-start | bytes 5898244
  361.8 6.7 %copy-start.7 = (bf16[1,2560,384]{2,1,0:T(8,128)(2,1)S(1)}, bf16[1,2560,384]{2,1,0:T(8,128)(2,1)}, u32[]{:S(2)}) copy-start(bf16[1,2560,384]{2,1,0:T(8,128)(2,1)} %param.20) | copy-start | bytes 5898244
  374.3 5.8 copy-start.4
  374.3 5.9 copy-start.3
  374.3 160.0 %all-to-all-start.2 = ((bf16[8,120,2560]{2,1,0:T(8,128)(2,1)}), bf16[8,120,2560]{2,1,0:T(8,128)(2,1)}, u32[]{:S(2)}, u32[]{:S(2)}) async-start(bf16[8,120,2560]{2,1,0:T(8,128)(2,1)} %bitcast.73), calls=%async_computation.2 | async-start | bytes 9830400 | tf_op jit(solution)/shard_map/all_to_all | solution.py:80
  379.1 188.4 %all-gather.6.cloned.1.call-start = ((), (), s32[]{:S(2)}) async-start(), calls=%async_computation.6 | async-start | bytes 4423680 | tf_op jit(solution)/shard_map/all_gather | solution.py:70
  379.8 219.4 %reduce-scatter.3.cloned.1.call-start = ((), (), s32[]{:S(2)}) async-start(), calls=%async_computation.8 | async-start | bytes 1966080 | tf_op jit(solution)/shard_map/reduce_scatter | solution.py:98
  574.1 8.9 %copy-start.8 = (u32[32]{0:T(128)S(1)}, u32[32]{0:T(128)}, u32[]{:S(2)}) copy-start(u32[32]{0:T(128)} %constant.51) | copy-start | bytes 388
  578.7 22.3 %copy-start.1 = (bf16[1,2560,384]{2,1,0:T(8,128)(2,1)S(1)}, bf16[1,2560,384]{2,1,0:T(8,128)(2,1)}, u32[]{:S(2)}) copy-start(bf16[1,2560,384]{2,1,0:T(8,128)(2,1)} %param.22) | copy-start | bytes 5898244
  579.4 9.9 %all-to-all-start.3 = ((bf16[8,1,120]{2,1,0:T(2,128)(2,1)}), bf16[8,1,120]{2,1,0:T(2,128)(2,1)S(1)}, u32[]{:S(2)}, u32[]{:S(2)}) async-start(bf16[8,1,120]{2,1,0:T(2,128)(2,1)} %convert_element_type.79), calls=%async_computation.4 | async-start | bytes 8192 | tf_op jit(solution)/shard_map/all_to_all | solution.py:81
Sparse Core Ops, SparseCore 0:
  48.6 144.1 all-gather.7
  209.5 143.2 all-gather.3
  382.1 143.1 all-gather.5
  578.9 7.6 reduce-scatter.2
where the time goes:
time: 608 us
  waiting for transfers between devices  453 us (75%)
  local copies, waits for them, and re-layouts  62.3 us (10%)
  matrix products  42.6 us (7%)
  starting transfers between devices  20.5 us (3%)
  between operations  14.7 us (2%)
  other arithmetic  11.4 us (2%)
    all_to_all x1, waiting for transfers between devices, body(): lax.all_to_all(send_x, 'exp', split_axis=0, concat_axis=0, tiled=True)  156 us
    all_to_all x1, waiting for transfers between devices, body(): lax.all_to_all(pieces, 'exp', split_axis=0, concat_axis=0, tiled=True)  148 us
    all_to_all x1, waiting for transfers between devices, body(): lax.all_to_all(send_dy, 'exp', split_axis=0, concat_axis=0, tiled=True)  141 us
    gather x6, local copies, waits for them, and re-layouts, body(): picked = jnp.take(flat_rows, slot_table[:, column], axis=0)  33.2 us
  transfers between devices with their start and end apart: 8, of which 4 were waited for; matrix products, arithmetic and copies ran while one was open for 12% of the time, Pallas kernels for 0%

commit v1 on v0

--- a/solution.py
+++ b/solution.py
@@ -1,7 +1,379 @@
+import functools
 import jax
 import jax.numpy as jnp
 from jax import lax
+from jax.experimental import pallas as pl
+from jax.experimental.pallas import tpu as pltpu
 from jax.sharding import PartitionSpec as P
+
+MESH = pl.DeviceIdType.MESH
+LANE = 128
+
+
+def ceil_lanes(count):
+    return (count + LANE - 1) // LANE * LANE
+
+
+def kernel(
+    n, x_ref, dy_ref, ids_ref, gates_ref, wg_ref, wu_ref, wd_ref, shared_ref,
+    out_ref, gg_ref,
+    tok, weights, pair_out, pair_in, sum_out, sum_in,
+    local_sem, tok_send, tok_recv, sib_send, sib_recv, pair_send, pair_recv,
+    sum_send, sum_recv, w_send, w_recv, fw_send, fw_recv,
+):
+    rows, depth = x_ref.shape
+    units = wg_ref.shape[2]
+    top = ids_ref.shape[1]
+    shared_rows = shared_ref.shape[1]
+    part_rows = shared_rows // 2
+    swide = shared_ref.shape[2] // 3
+    half = depth // 2
+    half_rows = rows // 2
+    x_wide = 2 * units + 2 * swide
+    shared_at = 2 * units
+    down_at = x_wide
+    grp, exp, core = lax.axis_index("grp"), lax.axis_index("exp"), lax.axis_index("sp")
+    other_grp, other_core = 1 - grp, 1 - core
+
+    side, along = exp % 2, exp // 2
+    place = (1 - side) * along + side * (n - 1 - along)
+
+    def device_at(where):
+        back = where // (n // 2)
+        return (1 - back) * (2 * where) + back * (2 * (n - 1 - where) + 1)
+
+    onward = (device_at((place + 1) % n), device_at((place + n - 1) % n))
+
+    loads = [
+        (x_ref, tok.at[0, 0, :, pl.ds(0, depth)]),
+        (dy_ref, tok.at[0, 1, :, pl.ds(0, depth)]),
+        (wg_ref.at[0], weights.at[:, pl.ds(0, units)]),
+        (wu_ref.at[0], weights.at[:, pl.ds(units, units)]),
+        (wd_ref.at[0], weights.at[:, pl.ds(down_at + swide, units)]),
+        (
+            shared_ref.at[exp],
+            weights.at[pl.ds(exp * shared_rows, shared_rows), pl.ds(shared_at, 3 * swide)],
+        ),
+    ]
+    loads = [
+        pltpu.make_async_copy(src, dst, local_sem.at[i]) for i, (src, dst) in enumerate(loads)
+    ]
+    for load in loads:
+        load.start()
+
+    barrier = pltpu.get_barrier_semaphore()
+    for k in range(1, n):
+        pl.semaphore_signal(
+            barrier, inc=1, device_id={"exp": (exp + k) % n}, device_id_type=MESH
+        )
+    pl.semaphore_signal(barrier, inc=1, device_id={"sp": other_core}, device_id_type=MESH)
+    pl.semaphore_signal(barrier, inc=1, device_id={"grp": other_grp}, device_id_type=MESH)
+
+    lane = lax.broadcasted_iota(jnp.int32, (rows, LANE), 1)
+    factor = jnp.zeros((rows, LANE), jnp.float32)
+    for k in range(top):
+        hit = (lane % n == ids_ref[:, k : k + 1]) & (lane < 3 * n)
+        factor = factor + jnp.where(hit, gates_ref[:, k : k + 1], 0.0)
+    first = factor.astype(jnp.bfloat16).astype(jnp.float32)
+    second = (factor - first).astype(jnp.bfloat16).astype(jnp.float32)
+    third = factor - first - second
+    terms = jnp.where(lane < n, first, jnp.where(lane < 2 * n, second, third))
+    tok[0, 0, :, pl.ds(depth, LANE)] = terms.astype(jnp.bfloat16)
+    tok[0, 1, :, pl.ds(depth, LANE)] = jnp.zeros((rows, LANE), jnp.bfloat16)
+
+    loads[0].wait()
+    loads[1].wait()
+    pl.semaphore_wait(barrier, n + 1)
+
+    def token_copy(step, way):
+        part = pl.ds(way * half_rows, half_rows)
+        return pltpu.make_async_remote_copy(
+            src_ref=tok.at[step, core, part],
+            dst_ref=tok.at[step + 1, core, part],
+            send_sem=tok_send.at[way, step],
+            recv_sem=tok_recv.at[way, step + 1],
+            device_id={"exp": onward[way]},
+            device_id_type=MESH,
+        )
+
+    def token_arrival(step, way):
+        part = pl.ds(way * half_rows, half_rows)
+        return pltpu.make_async_remote_copy(
+            src_ref=tok.at[step, core, part],
+            dst_ref=tok.at[step, core, part],
+            send_sem=tok_send.at[way, step],
+            recv_sem=tok_recv.at[way, step],
+            device_id={"exp": onward[way]},
+            device_id_type=MESH,
+        )
+
+    def sibling_copy(step, which):
+        return pltpu.make_async_remote_copy(
+            src_ref=tok.at[step, which],
+            dst_ref=tok.at[step, which],
+            send_sem=sib_send.at[step],
+            recv_sem=sib_recv.at[step],
+            device_id={"sp": other_core},
+            device_id_type=MESH,
+        )
+
+    def pair_copy(step):
+        return pltpu.make_async_remote_copy(
+            src_ref=pair_out.at[step],
+            dst_ref=pair_in.at[step],
+            send_sem=pair_send.at[step],
+            recv_sem=pair_recv.at[step],
+            device_id={"sp": other_core},
+            device_id_type=MESH,
+        )
+
+    def sum_copy(step, way):
+        part = pl.ds(way * half_rows, half_rows)
+        return pltpu.make_async_remote_copy(
+            src_ref=sum_out.at[step, part],
+            dst_ref=sum_in.at[step, part],
+            send_sem=sum_send.at[way, step],
+            recv_sem=sum_recv.at[way, step],
+            device_id={"exp": onward[way]},
+            device_id_type=MESH,
+        )
+
+    def shared_block(owner, part):
+        return weights.at[
+            pl.ds(owner * shared_rows + part * part_rows, part_rows),
+            pl.ds(shared_at, 3 * swide),
+        ]
+
+    def weight_copy(k):
+        target = (exp + k) % n
+        return pltpu.make_async_remote_copy(
+            src_ref=shared_ref.at[target, pl.ds(grp * part_rows, part_rows)],
+            dst_ref=shared_block(exp, grp),
+            send_sem=w_send.at[k],
+            recv_sem=w_recv.at[k],
+            device_id={"exp": target},
+            device_id_type=MESH,
+        )
+
+    def weight_arrival(k):
+        block = shared_block((exp + n - k) % n, grp)
+        return pltpu.make_async_remote_copy(
+            src_ref=block,
+            dst_ref=block,
+            send_sem=w_send.at[k],
+            recv_sem=w_recv.at[k],
+            device_id={"exp": (exp + k) % n},
+            device_id_type=MESH,
+        )
+
+    def weight_forward(k, part):
+        block = shared_block((exp + n - k) % n, part)
+        return pltpu.make_async_remote_copy(
+            src_ref=block,
+            dst_ref=block,
+            send_sem=fw_send.at[k],
+            recv_sem=fw_recv.at[k],
+            device_id={"grp": other_grp},
+            device_id_type=MESH,
+        )
+
+    for way in range(2):
+        token_copy(0, way).start()
+    for k in range(1, n):
+        weight_copy(k).start()
+
+    def back(grads, start, first_unit, unit_count):
+        return lax.dot_general(
+            grads,
+            weights[pl.ds(start, half), pl.ds(first_unit, unit_count)],
+            (((1,), (1,)), ((), ())),
+            preferred_element_type=jnp.float32,
+        )
+
+    def grads_of(gate_pre, up_pre, grad_out):
+        sigmoid_val = jax.nn.sigmoid(gate_pre)
+        silu_val = gate_pre * sigmoid_val
+        grad_gate = grad_out * up_pre * sigmoid_val * (1.0 + gate_pre * (1.0 - sigmoid_val))
+        grad_up = grad_out * silu_val
+        return (
+            jnp.concatenate(
+                [grad_gate.astype(jnp.bfloat16), grad_up.astype(jnp.bfloat16)], axis=1
+            ),
+            silu_val * up_pre,
+        )
+
+    def contribution(step):
+        forward = jnp.dot(
+            tok[step, 0, :, pl.ds(0, depth)],
+            weights[:, pl.ds(0, x_wide)],
+            preferred_element_type=jnp.float32,
+        )
+        down = jnp.dot(
+            tok[step, 1, :, pl.ds(0, depth)],
+            weights[:, pl.ds(down_at, swide + units)],
+            preferred_element_type=jnp.float32,
+        )
+        grad_out = down[:, swide:]
+        routed, hidden = grads_of(forward[:, :units], forward[:, units : 2 * units], grad_out)
+        shared, unused = grads_of(
+            forward[:, shared_at : shared_at + swide],
+            forward[:, shared_at + swide :],
+            down[:, :swide],
+        )
+        gate_part = jnp.sum(grad_out * hidden, axis=1, keepdims=True)
+        gate_part = gate_part.astype(jnp.bfloat16).astype(jnp.float32)
+        terms = tok[step, 0, :, pl.ds(depth, LANE)].astype(jnp.float32)
+        mine = (lane % n == exp) & (lane < 3 * n)
+        scale = jnp.sum(jnp.where(mine, terms, 0.0), axis=1, keepdims=True)
+
+        def columns(start):
+            return scale * back(routed, start, 0, 2 * units) + back(
+                shared, start, shared_at, 2 * swide
+            )
+
+        extra = jnp.where(lane == exp + n * core, gate_part, 0.0)
+        pair_out[step, :, pl.ds(0, half)] = columns(other_core * half)
+        pair_out[step, :, pl.ds(half, LANE)] = extra
+        pair_copy(step).start()
+        return columns(core * half), extra
+
+    def one_step(step, carry):
+        for way in range(2):
+            token_arrival(step, way).wait_recv()
+
+        @pl.when(step < n - 1)
+        def _():
+            for way in range(2):
+                token_copy(step, way).start()
+
+        sibling_copy(step, core).start()
+
+        @pl.when(step == 1)
+        def _():
+            for k in range(1, n):
+                weight_arrival(k).wait_recv()
+                weight_forward(k, grp).start()
+            for load in loads[2:]:
+                load.wait()
+            for k in range(1, n):
+                weight_forward(k, other_grp).wait_recv()
+
+        sibling_copy(step, other_core).wait_recv()
+        kept, extra = contribution(step)
+        pair_copy(step).wait_recv()
+        wide = pl.ds(0, half)
+        tail = pl.ds(half, LANE)
+        kept = kept + pair_in[step, :, wide]
+        extra = extra + pair_in[step, :, tail]
+
+        @pl.when(step == 1)
+        def _():
+            sum_out[step, :, wide] = kept.astype(jnp.bfloat16)
+            sum_out[step, :, tail] = extra.astype(jnp.bfloat16)
+
+        @pl.when(step > 1)
+        def _():
+            for way in range(2):
+                sum_copy(step - 1, way).wait_recv()
+            total = kept + sum_in[step - 1, :, wide].astype(jnp.float32)
+            sum_out[step, :, wide] = total.astype(jnp.bfloat16)
+            total = extra + sum_in[step - 1, :, tail].astype(jnp.float32)
+            sum_out[step, :, tail] = total.astype(jnp.bfloat16)
+
+        for way in range(2):
+            sum_copy(step, way).start()
+        return carry
+
+    lax.fori_loop(1, n, one_step, 0)
+
+    kept, extra = contribution(0)
+    pair_copy(0).wait_recv()
+    for way in range(2):
+        sum_copy(n - 1, way).wait_recv()
+    wide = pl.ds(0, half)
+    tail = pl.ds(half, LANE)
+    total = kept + pair_in[0, :, wide] + sum_in[n - 1, :, wide].astype(jnp.float32)
+    out_ref[...] = total.astype(jnp.bfloat16)
+    extra = extra + pair_in[0, :, tail] + sum_in[n - 1, :, tail].astype(jnp.float32)
+    for k in range(top // 2):
+        wanted = jnp.where(core == 0, ids_ref[:, k : k + 1], ids_ref[:, k + top // 2 : k + top // 2 + 1])
+        hit = (lane % n == wanted) & (lane < 2 * n)
+        gg_ref[:, k : k + 1] = jnp.sum(jnp.where(hit, extra, 0.0), axis=1, keepdims=True)
+
+    for k in range(1, n):
+        weight_copy(k).wait_send()
+        weight_forward(k, grp).wait_send()
+    pair_copy(0).wait_send()
+    for way in range(2):
+        token_copy(0, way).wait_send()
+
+    def drain(step, carry):
+        @pl.when(step < n - 1)
+        def _():
+            for way in range(2):
+                token_copy(step, way).wait_send()
+
+        sibling_copy(step, core).wait_send()
+        pair_copy(step).wait_send()
+        for way in range(2):
+            sum_copy(step, way).wait_send()
+        return carry
+
+    lax.fori_loop(1, n, drain, 0)
+
+
+def pack_shared(weight, n):
+    row_count, unit_count = weight.shape
+    share = unit_count // n
+    blocks = jnp.swapaxes(weight.reshape(row_count, n, share), 0, 1)
+    return jnp.pad(blocks, ((0, 0), (0, 0), (0, ceil_lanes(share) - share)))
+
+
+def fused_body(
+    tokens, cotangent, expert_ids, slot_ids, gates, w_gate, w_up, w_down, s_gate, s_up, s_down
+):
+    del slot_ids
+    n = lax.axis_size("exp")
+    rows, depth = tokens.shape
+    units = w_gate.shape[2]
+    top = expert_ids.shape[1]
+    shared = jnp.concatenate([pack_shared(w, n) for w in (s_gate, s_up, s_down)], axis=2)
+    swide = shared.shape[2] // 3
+    half = depth // 2
+    anywhere = pl.BlockSpec(memory_space=pl.ANY)
+    vmem = pl.BlockSpec(memory_space=pltpu.VMEM)
+    dma = pltpu.SemaphoreType.DMA
+    flops = 2 * n * rows * depth * 5 * (units + swide)
+    return pl.pallas_call(
+        functools.partial(kernel, n),
+        out_shape=(
+            jax.ShapeDtypeStruct((rows, half), jnp.bfloat16),
+            jax.ShapeDtypeStruct((rows, top // 2), jnp.float32),
+        ),
+        in_specs=[anywhere, anywhere, vmem, vmem] + [anywhere] * 4,
+        out_specs=(vmem, vmem),
+        scratch_shapes=[
+            pltpu.VMEM((n, 2, rows, depth + LANE), jnp.bfloat16),
+            pltpu.VMEM((depth, 3 * units + 3 * swide), jnp.bfloat16),
+            pltpu.VMEM((n, rows, half + LANE), jnp.float32),
+            pltpu.VMEM((n, rows, half + LANE), jnp.float32),
+            pltpu.VMEM((n, rows, half + LANE), jnp.bfloat16),
+            pltpu.VMEM((n, rows, half + LANE), jnp.bfloat16),
+            dma((6,)),
+            dma((2, n)), dma((2, n)),
+            dma((n,)), dma((n,)),
+            dma((n,)), dma((n,)),
+            dma((2, n)), dma((2, n)),
+            dma((n,)), dma((n,)),
+            dma((n,)), dma((n,)),
+        ],
+        compiler_params=pltpu.CompilerParams(
+            collective_id=0, has_side_effects=True, vmem_limit_bytes=56 * 1024 * 1024
+        ),
+        cost_estimate=pl.CostEstimate(
+            flops=flops, bytes_accessed=32 * 1024 * 1024, transcendentals=0
+        ),
+    )(tokens, cotangent, expert_ids, gates, w_gate, w_up, w_down, shared)
 
 
 def swiglu_grads(gate_pre, up_pre, grad_out):
@@ -116,4 +488,6 @@
         P("exp", "sp"),
     )
     out_specs = (P(("grp", "exp"), "sp"), P(("grp", "exp"), "sp"))
-    return jax.shard_map(body, mesh=mesh, in_specs=in_specs, out_specs=out_specs, check_vma=False)
+    fused = mesh.shape["grp"] == 2 and mesh.shape["sp"] == 2 and mesh.shape["exp"] == 8
+    chosen = fused_body if fused else body
+    return jax.shard_map(chosen, mesh=mesh, in_specs=in_specs, out_specs=out_specs, check_vma=False)

time: 608 us -> 133 us (0.22)
  waiting for transfers between devices: 453 us -> 0 us
  Pallas kernels: 0 us -> 123 us
  local copies, waits for them, and re-layouts: 62.3 us -> 7.73 us
  matrix products: 42.6 us -> 0 us
  starting transfers between devices: 20.5 us -> 0 us
  between operations: 14.7 us -> 0.7 us
  other arithmetic: 11.4 us -> 1.71 us
    all_to_all x4 -> x0, waiting for transfers between devices: 450 us -> none  [the longest x1 156 us: body(): lax.all_to_all(send_x, 'exp', split_axis=0, concat_axis=0, tiled=True)]
    pallas_call x0 -> x1, Pallas kernels: none -> 123 us  [fused_body(): pl.pallas_call(functools.partial(kernel, n), out_shape=(jax.ShapeDtypeStr...]
    gather x11 -> x0, local copies, waits for them, and re-layouts: 56.2 us -> none  [the longest x6 33.2 us: body(): picked = jnp.take(flat_rows, slot_table[:, column], axis=0)]
    dot_general x8 -> x0, matrix products: 42.6 us -> none  [the longest x2 11.2 us: contract_back(): lax.dot_general(grads, weight, (((1,), (1,)), ((), ())), preferred_elemen...]
    all_to_all x4 -> x0, starting transfers between devices: 20.2 us -> none  [the longest x1 7.29 us: body(): lax.all_to_all(send_x, 'exp', split_axis=0, concat_axis=0, tiled=True)]
    select_n x3 -> x0, other arithmetic: 8.62 us -> none  [the longest x1 8.59 us: body(): jnp.take(tokens, slot_owner, axis=0)]
  transfers between devices with their start and end apart: 8 -> 0, of which waited for: 4 -> 0; matrix products, arithmetic and copies ran while one was open for 12% -> 0% of each run, Pallas kernels for 0% -> 0%
where the time goes in v1:
time: 133 us
  Pallas kernels  123 us (92%)
  local copies, waits for them, and re-layouts  7.73 us (6%)
  other arithmetic  1.71 us (1%)
    pallas_call x1, Pallas kernels, fused_body(): pl.pallas_call(functools.partial(kernel, n), out_shape=(jax.ShapeDtypeStr...  123 us
    unnamed x14, local copies, waits for them, and re-layouts  5.21 us

profile of v1, /device:TPU:0, one launch (start us, length us, event | category | flops | bytes accessed | tf_op | source)
XLA Modules:
  0.0 133.0 jit_solution(6288915999808659726)
XLA Ops:
  0.6 0.0 copy-start
  0.6 1.4 %copy.15 = bf16[320,768]{0,1:T(8,128)(2,1)S(1)} copy(bf16[320,768]{1,0:T(8,128)(2,1)} %param.18) | data formatting | bytes 983040 | tf_op args[8]
  2.0 0.0 copy-start.1
  2.0 0.3 copy.16
  2.4 0.0 copy-done
  2.4 0.3 copy.17
  2.7 0.3 copy.18
  3.1 0.0 copy-done.1
  3.1 0.3 copy.19
  3.4 0.3 copy.20
  3.7 0.0 copy-start.2
  3.7 0.0 copy-start.3
  3.7 1.7 %fusion.5.shared_ref = bf16[8,320,384]{2,1,0:T(8,128)(2,1)} fusion(bf16[8,320,96]{2,1,0:T(8,128)(2,1)S(1)} %bitcast.8, bf16[8,320,96]{2,1,0:T(8,128)(2,1)S(1)} %bitcast.7, bf16[8,320,96]{2,1,0:T(8,128)(2,1)S(1)} %bitcast.6), kind=kLoop, calls=%fused_computation.9 | loop fusion | flops 13762560 | bytes 3440640 | tf_op jit(solution)/shard_map/concatenate | solution.py:340
  5.5 0.0 copy-done.2
  5.5 0.7 copy.21.ids_ref
  6.2 0.0 copy-done.3
  6.2 0.7 copy.22.gates_ref
  6.9 122.8 %shard_map.113 = (bf16[128,1280]{1,0:T(8,128)(2,1)}, f32[128,3]{1,0:T(8,128)}) custom-call(bf16[128,2560]{1,0:T(8,128)(2,1)} %x_ref.1, bf16[128,2560]{1,0:T(8,128)(2,1)} %dy_ref.1, s32[128,6]{1,0:T(8,128)} %copy.21.ids_ref, f32[128,6]{1,0:T(8,128)} %copy.22.gates_ref, bf16[1,2560,384]{2,1,0:T(8,128)(2,1)} %wg_ref.1, bf16[1,2560,384]{2,1,0:T(8,128)(2,1)} %wu_ref.1, ...), custom_call_target="tpu_custom_call" | custom-call | flops 13421772800 | bytes 33554432 | tf_op jit(solution)/shard_map/pallas_call | solution.py:347
  129.8 1.5 %copy.23 = f32[128,3]{0,1:T(4,128)} copy(f32[128,3]{1,0:T(8,128)} %get-tuple-element.5) | data formatting | bytes 3072 | tf_op jit(solution)/shard_map/pallas_call | solution.py:347
  131.3 1.7 %copy.25 = bf16[128,1280]{1,0:T(8,128)(2,1)} copy(bf16[128,1280]{1,0:T(8,128)(2,1)} %get-tuple-element.8) | data formatting | bytes 655360
Async XLA Ops:
  0.6 1.8 %copy-start = (bf16[320,768]{1,0:T(8,128)(2,1)S(1)}, bf16[320,768]{1,0:T(8,128)(2,1)}, u32[]{:S(2)}) copy-start(bf16[320,768]{1,0:T(8,128)(2,1)} %param.19) | copy-start | bytes 1474564
  2.0 1.0 copy-start.1
  3.7 1.7 %copy-start.2 = (s32[128,6]{0,1:T(8,128)S(1)}, s32[128,6]{0,1:T(8,128)}, u32[]{:S(2)}) copy-start(s32[128,6]{0,1:T(8,128)} %param.13) | copy-start | bytes 9220
  3.7 2.5 %copy-start.3 = (f32[128,6]{0,1:T(8,128)S(1)}, f32[128,6]{0,1:T(8,128)}, u32[]{:S(2)}) copy-start(f32[128,6]{0,1:T(8,128)} %param.14) | copy-start | bytes 9220

commit v2 on v1

--- a/solution.py
+++ b/solution.py
@@ -8,6 +8,7 @@
 
 MESH = pl.DeviceIdType.MESH
 LANE = 128
+EAGER = 1
 
 
 def ceil_lanes(count):
@@ -15,16 +16,19 @@
 
 
 def kernel(
-    n, x_ref, dy_ref, ids_ref, gates_ref, wg_ref, wu_ref, wd_ref, shared_ref,
+    n, x_ref, dy_ref, ids_ref, gates_ref, wg_ref, wu_ref, wd_ref, sg_ref, su_ref, sd_ref,
     out_ref, gg_ref,
-    tok, weights, pair_out, pair_in, sum_out, sum_in,
+    tok, weights, shared_in, shared_ref, pair_out, pair_in, sum_out, sum_in,
+    factor_out, factor_in, gate_out, gate_in,
     local_sem, tok_send, tok_recv, sib_send, sib_recv, pair_send, pair_recv,
     sum_send, sum_recv, w_send, w_recv, fw_send, fw_recv,
+    factor_send, factor_recv, gate_send, gate_recv,
 ):
     rows, depth = x_ref.shape
     units = wg_ref.shape[2]
-    top = ids_ref.shape[1]
+    top = ids_ref.shape[0]
     shared_rows = shared_ref.shape[1]
+    share = sg_ref.shape[1] // n
     part_rows = shared_rows // 2
     swide = shared_ref.shape[2] // 3
     half = depth // 2
@@ -45,15 +49,14 @@
     onward = (device_at((place + 1) % n), device_at((place + n - 1) % n))
 
     loads = [
-        (x_ref, tok.at[0, 0, :, pl.ds(0, depth)]),
-        (dy_ref, tok.at[0, 1, :, pl.ds(0, depth)]),
+        (x_ref, tok.at[0, 0]),
+        (dy_ref, tok.at[0, 1]),
+        (sg_ref, shared_in.at[0]),
+        (su_ref, shared_in.at[1]),
+        (sd_ref, shared_in.at[2]),
         (wg_ref.at[0], weights.at[:, pl.ds(0, units)]),
         (wu_ref.at[0], weights.at[:, pl.ds(units, units)]),
         (wd_ref.at[0], weights.at[:, pl.ds(down_at + swide, units)]),
-        (
-            shared_ref.at[exp],
-            weights.at[pl.ds(exp * shared_rows, shared_rows), pl.ds(shared_at, 3 * swide)],
-        ),
     ]
     loads = [
         pltpu.make_async_copy(src, dst, local_sem.at[i]) for i, (src, dst) in enumerate(loads)
@@ -69,17 +72,13 @@
     pl.semaphore_signal(barrier, inc=1, device_id={"sp": other_core}, device_id_type=MESH)
     pl.semaphore_signal(barrier, inc=1, device_id={"grp": other_grp}, device_id_type=MESH)
 
-    lane = lax.broadcasted_iota(jnp.int32, (rows, LANE), 1)
-    factor = jnp.zeros((rows, LANE), jnp.float32)
-    for k in range(top):
-        hit = (lane % n == ids_ref[:, k : k + 1]) & (lane < 3 * n)
-        factor = factor + jnp.where(hit, gates_ref[:, k : k + 1], 0.0)
-    first = factor.astype(jnp.bfloat16).astype(jnp.float32)
-    second = (factor - first).astype(jnp.bfloat16).astype(jnp.float32)
-    third = factor - first - second
-    terms = jnp.where(lane < n, first, jnp.where(lane < 2 * n, second, third))
-    tok[0, 0, :, pl.ds(depth, LANE)] = terms.astype(jnp.bfloat16)
-    tok[0, 1, :, pl.ds(depth, LANE)] = jnp.zeros((rows, LANE), jnp.bfloat16)
+    row_lane = lax.broadcasted_iota(jnp.int32, (8, rows), 1)
+    for i in range(n):
+        factor = jnp.zeros((1, rows), jnp.float32)
+        for k in range(top):
+            factor = factor + jnp.where(ids_ref[k : k + 1, :] == i, gates_ref[k : k + 1, :], 0.0)
+        factor_out[i] = jnp.broadcast_to(factor, (8, rows))
+    factor_in[exp] = factor_out[exp]
 
     loads[0].wait()
     loads[1].wait()
@@ -177,10 +176,71 @@
             device_id_type=MESH,
         )
 
+    def factor_copy(k):
+        target = (exp + k) % n
+        return pltpu.make_async_remote_copy(
+            src_ref=factor_out.at[target],
+            dst_ref=factor_in.at[exp],
+            send_sem=factor_send.at[k],
+            recv_sem=factor_recv.at[k],
+            device_id={"exp": target},
+            device_id_type=MESH,
+        )
+
+    def factor_arrival(k):
+        return pltpu.make_async_remote_copy(
+            src_ref=factor_out.at[(exp + k) % n],
+            dst_ref=factor_in.at[(exp + n - k) % n],
+            send_sem=factor_send.at[k],
+            recv_sem=factor_recv.at[k],
+            device_id={"exp": (exp + k) % n},
+            device_id_type=MESH,
+        )
+
+    def behind(step, way):
+        return device_at((place + n - step) % n if way == 0 else (place + step) % n)
+
+    def gate_copy(step, way):
+        return pltpu.make_async_remote_copy(
+            src_ref=gate_out.at[step],
+            dst_ref=gate_in.at[way, exp],
+            send_sem=gate_send.at[way, step],
+            recv_sem=gate_recv.at[way, step],
+            device_id={"exp": behind(step, way)},
+            device_id_type=MESH,
+        )
+
+    def gate_arrival(step, way):
+        return pltpu.make_async_remote_copy(
+            src_ref=gate_out.at[step],
+            dst_ref=gate_in.at[way, behind(step, 1 - way)],
+            send_sem=gate_send.at[way, step],
+            recv_sem=gate_recv.at[way, step],
+            device_id={"exp": behind(step, way)},
+            device_id_type=MESH,
+        )
+
     for way in range(2):
         token_copy(0, way).start()
     for k in range(1, n):
+        factor_copy(k).start()
+    for load in loads[2:5]:
+        load.wait()
+    for i in range(n):
+        for j in range(3):
+            piece = shared_in[j, :, i * share : (i + 1) * share]
+            if swide > share:
+                blank = jnp.zeros((shared_rows, swide - share), jnp.bfloat16)
+                piece = jnp.concatenate([piece, blank], axis=1)
+            shared_ref[i, :, pl.ds(j * swide, swide)] = piece
+    for k in range(1, n):
         weight_copy(k).start()
+    own_shared = pltpu.make_async_copy(
+        shared_ref.at[exp],
+        weights.at[pl.ds(exp * shared_rows, shared_rows), pl.ds(shared_at, 3 * swide)],
+        local_sem.at[8],
+    )
+    own_shared.start()
 
     def back(grads, start, first_unit, unit_count):
         return lax.dot_general(
@@ -204,12 +264,12 @@
 
     def contribution(step):
         forward = jnp.dot(
-            tok[step, 0, :, pl.ds(0, depth)],
+            tok[step, 0],
             weights[:, pl.ds(0, x_wide)],
             preferred_element_type=jnp.float32,
         )
         down = jnp.dot(
-            tok[step, 1, :, pl.ds(0, depth)],
+            tok[step, 1],
             weights[:, pl.ds(down_at, swide + units)],
             preferred_element_type=jnp.float32,
         )
@@ -222,22 +282,26 @@
         )
         gate_part = jnp.sum(grad_out * hidden, axis=1, keepdims=True)
         gate_part = gate_part.astype(jnp.bfloat16).astype(jnp.float32)
-        terms = tok[step, 0, :, pl.ds(depth, LANE)].astype(jnp.float32)
-        mine = (lane % n == exp) & (lane < 3 * n)
-        scale = jnp.sum(jnp.where(mine, terms, 0.0), axis=1, keepdims=True)
+        upper = factor_in[behind(step, 0)]
+        lower = factor_in[behind(step, 1)]
+        scale = jnp.where(row_lane < half_rows, upper, lower)
+        scale = jnp.broadcast_to(scale[0:1], (rows, rows)).T[:, 0:1]
 
         def columns(start):
             return scale * back(routed, start, 0, 2 * units) + back(
                 shared, start, shared_at, 2 * swide
             )
 
-        extra = jnp.where(lane == exp + n * core, gate_part, 0.0)
+        extra = jnp.broadcast_to(gate_part, (rows, LANE))
         pair_out[step, :, pl.ds(0, half)] = columns(other_core * half)
         pair_out[step, :, pl.ds(half, LANE)] = extra
         pair_copy(step).start()
         return columns(core * half), extra
 
-    def one_step(step, carry):
+    wide = pl.ds(0, half)
+    tail = pl.ds(half, LANE)
+
+    def pass_on(step):
         for way in range(2):
             token_arrival(step, way).wait_recv()
 
@@ -248,61 +312,77 @@
 
         sibling_copy(step, core).start()
 
+    def one_step(step, carry):
+        @pl.when((step == 1) | (step > EAGER))
+        def _():
+            pass_on(step)
+
         @pl.when(step == 1)
         def _():
+            for early in range(2, EAGER + 1):
+                pass_on(early)
             for k in range(1, n):
                 weight_arrival(k).wait_recv()
                 weight_forward(k, grp).start()
-            for load in loads[2:]:
+            for load in loads[5:]:
                 load.wait()
+            own_shared.wait()
+            for k in range(1, n):
+                factor_arrival(k).wait_recv()
             for k in range(1, n):
                 weight_forward(k, other_grp).wait_recv()
 
         sibling_copy(step, other_core).wait_recv()
         kept, extra = contribution(step)
         pair_copy(step).wait_recv()
-        wide = pl.ds(0, half)
-        tail = pl.ds(half, LANE)
         kept = kept + pair_in[step, :, wide]
-        extra = extra + pair_in[step, :, tail]
 
         @pl.when(step == 1)
         def _():
-            sum_out[step, :, wide] = kept.astype(jnp.bfloat16)
-            sum_out[step, :, tail] = extra.astype(jnp.bfloat16)
+            sum_out[step] = kept.astype(jnp.bfloat16)
 
         @pl.when(step > 1)
         def _():
             for way in range(2):
                 sum_copy(step - 1, way).wait_recv()
-            total = kept + sum_in[step - 1, :, wide].astype(jnp.float32)
-            sum_out[step, :, wide] = total.astype(jnp.bfloat16)
-            total = extra + sum_in[step - 1, :, tail].astype(jnp.float32)
-            sum_out[step, :, tail] = total.astype(jnp.bfloat16)
+            total = kept + sum_in[step - 1].astype(jnp.float32)
+            sum_out[step] = total.astype(jnp.bfloat16)
 
         for way in range(2):
             sum_copy(step, way).start()
+        gate_out[step] = (extra + pair_in[step, :, tail]).T[0:8]
+        for way in range(2):
+            gate_copy(step, way).start()
         return carry
 
     lax.fori_loop(1, n, one_step, 0)
 
     kept, extra = contribution(0)
     pair_copy(0).wait_recv()
+    gate_own = (extra + pair_in[0, :, tail]).T[0:8]
+    gate_in[0, exp] = gate_own
+    gate_in[1, exp] = gate_own
+    for step in range(1, n):
+        for way in range(2):
+            gate_arrival(step, way).wait_recv()
+    for k in range(top // 2):
+        wanted = jnp.where(
+            core == 0, ids_ref[k : k + 1, :], ids_ref[k + top // 2 : k + top // 2 + 1, :]
+        )
+        total = jnp.zeros((1, rows), jnp.float32)
+        for i in range(n):
+            gate_row = jnp.where(row_lane < half_rows, gate_in[0, i], gate_in[1, i])[0:1]
+            total = total + jnp.where(wanted == i, gate_row, 0.0)
+        gg_ref[k : k + 1, :] = total
+    kept = kept + pair_in[0, :, wide]
     for way in range(2):
         sum_copy(n - 1, way).wait_recv()
-    wide = pl.ds(0, half)
-    tail = pl.ds(half, LANE)
-    total = kept + pair_in[0, :, wide] + sum_in[n - 1, :, wide].astype(jnp.float32)
-    out_ref[...] = total.astype(jnp.bfloat16)
-    extra = extra + pair_in[0, :, tail] + sum_in[n - 1, :, tail].astype(jnp.float32)
-    for k in range(top // 2):
-        wanted = jnp.where(core == 0, ids_ref[:, k : k + 1], ids_ref[:, k + top // 2 : k + top // 2 + 1])
-        hit = (lane % n == wanted) & (lane < 2 * n)
-        gg_ref[:, k : k + 1] = jnp.sum(jnp.where(hit, extra, 0.0), axis=1, keepdims=True)
+    out_ref[...] = (kept + sum_in[n - 1].astype(jnp.float32)).astype(jnp.bfloat16)
 
     for k in range(1, n):
         weight_copy(k).wait_send()
         weight_forward(k, grp).wait_send()
+        factor_copy(k).wait_send()
     pair_copy(0).wait_send()
     for way in range(2):
         token_copy(0, way).wait_send()
@@ -317,55 +397,56 @@
         pair_copy(step).wait_send()
         for way in range(2):
             sum_copy(step, way).wait_send()
+            gate_copy(step, way).wait_send()
         return carry
 
     lax.fori_loop(1, n, drain, 0)
-
-
-def pack_shared(weight, n):
-    row_count, unit_count = weight.shape
-    share = unit_count // n
-    blocks = jnp.swapaxes(weight.reshape(row_count, n, share), 0, 1)
-    return jnp.pad(blocks, ((0, 0), (0, 0), (0, ceil_lanes(share) - share)))
 
 
 def fused_body(
     tokens, cotangent, expert_ids, slot_ids, gates, w_gate, w_up, w_down, s_gate, s_up, s_down
 ):
-    del slot_ids
     n = lax.axis_size("exp")
     rows, depth = tokens.shape
     units = w_gate.shape[2]
     top = expert_ids.shape[1]
-    shared = jnp.concatenate([pack_shared(w, n) for w in (s_gate, s_up, s_down)], axis=2)
-    swide = shared.shape[2] // 3
+    shared_rows, shared_units = s_gate.shape
+    swide = ceil_lanes(shared_units // n)
     half = depth // 2
     anywhere = pl.BlockSpec(memory_space=pl.ANY)
     vmem = pl.BlockSpec(memory_space=pltpu.VMEM)
     dma = pltpu.SemaphoreType.DMA
     flops = 2 * n * rows * depth * 5 * (units + swide)
-    return pl.pallas_call(
+    input_grad, gate_grads = pl.pallas_call(
         functools.partial(kernel, n),
         out_shape=(
             jax.ShapeDtypeStruct((rows, half), jnp.bfloat16),
-            jax.ShapeDtypeStruct((rows, top // 2), jnp.float32),
+            jax.ShapeDtypeStruct((top // 2, rows), jnp.float32),
         ),
-        in_specs=[anywhere, anywhere, vmem, vmem] + [anywhere] * 4,
+        in_specs=[anywhere, anywhere, vmem, vmem] + [anywhere] * 6,
         out_specs=(vmem, vmem),
         scratch_shapes=[
-            pltpu.VMEM((n, 2, rows, depth + LANE), jnp.bfloat16),
+            pltpu.VMEM((n, 2, rows, depth), jnp.bfloat16),
             pltpu.VMEM((depth, 3 * units + 3 * swide), jnp.bfloat16),
+            pltpu.VMEM((3, shared_rows, shared_units), jnp.bfloat16),
+            pltpu.VMEM((n, shared_rows, 3 * swide), jnp.bfloat16),
             pltpu.VMEM((n, rows, half + LANE), jnp.float32),
             pltpu.VMEM((n, rows, half + LANE), jnp.float32),
-            pltpu.VMEM((n, rows, half + LANE), jnp.bfloat16),
-            pltpu.VMEM((n, rows, half + LANE), jnp.bfloat16),
-            dma((6,)),
+            pltpu.VMEM((n, rows, half), jnp.bfloat16),
+            pltpu.VMEM((n, rows, half), jnp.bfloat16),
+            pltpu.VMEM((n, 8, rows), jnp.float32),
+            pltpu.VMEM((n, 8, rows), jnp.float32),
+            pltpu.VMEM((n, 8, rows), jnp.float32),
+            pltpu.VMEM((2, n, 8, rows), jnp.float32),
+            dma((9,)),
             dma((2, n)), dma((2, n)),
             dma((n,)), dma((n,)),
             dma((n,)), dma((n,)),
             dma((2, n)), dma((2, n)),
             dma((n,)), dma((n,)),
             dma((n,)), dma((n,)),
+            dma((n,)), dma((n,)),
+            dma((2, n)), dma((2, n)),
         ],
         compiler_params=pltpu.CompilerParams(
             collective_id=0, has_side_effects=True, vmem_limit_bytes=56 * 1024 * 1024
@@ -373,7 +454,8 @@
         cost_estimate=pl.CostEstimate(
             flops=flops, bytes_accessed=32 * 1024 * 1024, transcendentals=0
         ),
-    )(tokens, cotangent, expert_ids, gates, w_gate, w_up, w_down, shared)
+    )(tokens, cotangent, expert_ids.T, gates.T, w_gate, w_up, w_down, s_gate, s_up, s_down)
+    return input_grad, gate_grads.T
 
 
 def swiglu_grads(gate_pre, up_pre, grad_out):

time: 133 us -> 125 us (0.940)
  local copies, waits for them, and re-layouts: 7.73 us -> 2.97 us
  Pallas kernels: 123 us -> 121 us
  other arithmetic: 1.71 us -> 0 us
    unnamed x14 -> x2, local copies, waits for them, and re-layouts: 5.21 us -> 2.97 us
    pallas_call x1, Pallas kernels: 123 us -> 121 us  [fused_body(): pl.pallas_call(functools.partial(kernel, n), out_shape=(jax.ShapeDtypeStr...]
    concatenate x1 -> x0, other arithmetic: 1.71 us -> none  [fused_body(): jnp.concatenate([pack_shared(w, n) for w in (s_gate, s_up, s_down)], axis=2)]
    pallas_call x1 -> x0, local copies, waits for them, and re-layouts: 1.49 us -> none  [fused_body(): pl.pallas_call(functools.partial(kernel, n), out_shape=(jax.ShapeDtypeStr...]
where the time goes in v2:
time: 125 us; the launch traced here: 124 us
  Pallas kernels  121 us (97%)
  local copies, waits for them, and re-layouts  2.97 us (2%)
    pallas_call x1, Pallas kernels, fused_body(): pl.pallas_call(functools.partial(kernel, n), out_shape=(jax.ShapeDtypeStr...  121 us
    unnamed x2, local copies, waits for them, and re-layouts  2.97 us

profile of v2, /device:TPU:0, one launch (start us, length us, event | category | flops | bytes accessed | tf_op | source)
XLA Modules:
  0.0 124.4 jit_solution(11356721034153317195)
XLA Ops:
  0.6 120.8 %shard_map.113 = (bf16[128,1280]{1,0:T(8,128)(2,1)}, f32[3,128]{1,0:T(4,128)}) custom-call(bf16[128,2560]{1,0:T(8,128)(2,1)} %x_ref.1, bf16[128,2560]{1,0:T(8,128)(2,1)} %dy_ref.1, s32[6,128]{1,0:T(8,128)} %bitcast.4, f32[6,128]{1,0:T(8,128)} %bitcast.5, bf16[1,2560,384]{2,1,0:T(8,128)(2,1)} %wg_ref.1, bf16[1,2560,384]{2,1,0:T(8,128)(2,1)} %wu_ref.1, ...), custom_call_target="tpu_custom_call" | custom-call | flops 13421772800 | bytes 33554432 | tf_op jit(solution)/shard_map/pallas_call | solution.py:420
  121.4 1.7 %copy.14 = bf16[128,1280]{1,0:T(8,128)(2,1)} copy(bf16[128,1280]{1,0:T(8,128)(2,1)} %get-tuple-element.8) | data formatting | bytes 655360
  123.1 1.3 %copy.15 = f32[128,3]{0,1:T(4,128)} copy(f32[128,3]{0,1:T(4,128)} %bitcast.3) | data formatting | bytes 3072

commit v3 on v2

--- a/solution.py
+++ b/solution.py
@@ -8,7 +8,6 @@
 
 MESH = pl.DeviceIdType.MESH
 LANE = 128
-EAGER = 1
 
 
 def ceil_lanes(count):
@@ -18,7 +17,7 @@
 def kernel(
     n, x_ref, dy_ref, ids_ref, gates_ref, wg_ref, wu_ref, wd_ref, sg_ref, su_ref, sd_ref,
     out_ref, gg_ref,
-    tok, weights, shared_in, shared_ref, pair_out, pair_in, sum_out, sum_in,
+    kept_buf, tok, weights, shared_in, shared_ref, pair_out, pair_in, sum_out, sum_in,
     factor_out, factor_in, gate_out, gate_in,
     local_sem, tok_send, tok_recv, sib_send, sib_recv, pair_send, pair_recv,
     sum_send, sum_recv, w_send, w_recv, fw_send, fw_recv,
@@ -312,30 +311,14 @@
 
         sibling_copy(step, core).start()
 
-    def one_step(step, carry):
-        @pl.when((step == 1) | (step > EAGER))
-        def _():
-            pass_on(step)
-
-        @pl.when(step == 1)
-        def _():
-            for early in range(2, EAGER + 1):
-                pass_on(early)
-            for k in range(1, n):
-                weight_arrival(k).wait_recv()
-                weight_forward(k, grp).start()
-            for load in loads[5:]:
-                load.wait()
-            own_shared.wait()
-            for k in range(1, n):
-                factor_arrival(k).wait_recv()
-            for k in range(1, n):
-                weight_forward(k, other_grp).wait_recv()
-
-        sibling_copy(step, other_core).wait_recv()
+    def prepare(step):
         kept, extra = contribution(step)
+        kept_buf[step % 2, :, wide] = kept
+        kept_buf[step % 2, :, tail] = extra
+
+    def finish(step):
         pair_copy(step).wait_recv()
-        kept = kept + pair_in[step, :, wide]
+        kept = kept_buf[step % 2, :, wide] + pair_in[step, :, wide]
 
         @pl.when(step == 1)
         def _():
@@ -350,15 +333,42 @@
 
         for way in range(2):
             sum_copy(step, way).start()
-        gate_out[step] = (extra + pair_in[step, :, tail]).T[0:8]
+        extra = kept_buf[step % 2, :, tail] + pair_in[step, :, tail]
+        gate_out[step] = extra.T[0:8]
         for way in range(2):
             gate_copy(step, way).start()
+
+    def one_step(step, carry):
+        @pl.when(step < n - 1)
+        def _():
+            pass_on(step + 1)
+
+        finish(step)
+
+        @pl.when(step < n - 1)
+        def _():
+            sibling_copy(step + 1, other_core).wait_recv()
+
+        prepare((step + 1) % n)
         return carry
 
+    pass_on(1)
+    for k in range(1, n):
+        weight_arrival(k).wait_recv()
+        weight_forward(k, grp).start()
+    for load in loads[5:]:
+        load.wait()
+    own_shared.wait()
+    for k in range(1, n):
+        factor_arrival(k).wait_recv()
+    for k in range(1, n):
+        weight_forward(k, other_grp).wait_recv()
+    sibling_copy(1, other_core).wait_recv()
+    prepare(1)
     lax.fori_loop(1, n, one_step, 0)
-
-    kept, extra = contribution(0)
     pair_copy(0).wait_recv()
+    kept = kept_buf[0, :, wide]
+    extra = kept_buf[0, :, tail]
     gate_own = (extra + pair_in[0, :, tail]).T[0:8]
     gate_in[0, exp] = gate_own
     gate_in[1, exp] = gate_own
@@ -426,6 +436,7 @@
         in_specs=[anywhere, anywhere, vmem, vmem] + [anywhere] * 6,
         out_specs=(vmem, vmem),
         scratch_shapes=[
+            pltpu.VMEM((2, rows, half + LANE), jnp.float32),
             pltpu.VMEM((n, 2, rows, depth), jnp.bfloat16),
             pltpu.VMEM((depth, 3 * units + 3 * swide), jnp.bfloat16),
             pltpu.VMEM((3, shared_rows, shared_units), jnp.bfloat16),

time: 125 us -> 120 us (0.960)
  Pallas kernels: 121 us -> 116 us
    pallas_call x1, Pallas kernels: 121 us -> 116 us  [fused_body(): pl.pallas_call(functools.partial(kernel, n), out_shape=(jax.ShapeDtypeStr...]
where the time goes in v3:
time: 120 us; the launch traced here: 119 us
  Pallas kernels  116 us (97%)
  local copies, waits for them, and re-layouts  2.97 us (2%)
    pallas_call x1, Pallas kernels, fused_body(): pl.pallas_call(functools.partial(kernel, n), out_shape=(jax.ShapeDtypeStr...  116 us
    unnamed x2, local copies, waits for them, and re-layouts  2.97 us

profile of v3, /device:TPU:0, one launch (start us, length us, event | category | flops | bytes accessed | tf_op | source)
XLA Modules:
  0.0 119.5 jit_solution(8654346042590576213)
XLA Ops:
  0.6 115.9 %shard_map.113 = (bf16[128,1280]{1,0:T(8,128)(2,1)}, f32[3,128]{1,0:T(4,128)}) custom-call(bf16[128,2560]{1,0:T(8,128)(2,1)} %x_ref.1, bf16[128,2560]{1,0:T(8,128)(2,1)} %dy_ref.1, s32[6,128]{1,0:T(8,128)} %bitcast.4, f32[6,128]{1,0:T(8,128)} %bitcast.5, bf16[1,2560,384]{2,1,0:T(8,128)(2,1)} %wg_ref.1, bf16[1,2560,384]{2,1,0:T(8,128)(2,1)} %wu_ref.1, ...), custom_call_target="tpu_custom_call" | custom-call | flops 13421772800 | bytes 33554432 | tf_op jit(solution)/shard_map/pallas_call | solution.py:430
  116.5 1.7 %copy.14 = bf16[128,1280]{1,0:T(8,128)(2,1)} copy(bf16[128,1280]{1,0:T(8,128)(2,1)} %get-tuple-element.8) | data formatting | bytes 655360
  118.2 1.3 %copy.15 = f32[128,3]{0,1:T(4,128)} copy(f32[128,3]{0,1:T(4,128)} %bitcast.3) | data formatting | bytes 3072
